TPU v7x, 32 devices: a whole 2x2x4 slice. The times are simulated.
32 devices in a mesh: segment: 2 (over x), dp: 4 (over z), mp: 4 (over y, core).
Axes of the slice: x: 2, y: 2, z: 4, core: 2. Of those that a mesh axis runs over, the one named last changes fastest.
Arguments:
- patch_tokens: bfloat16 [32, 16, 3072], P('dp', None, 'mp'), may hold values from -400 to 400
- visible_index: int32 [32, 16], P('dp'), may hold values from 0 to 63, as said below
- output_grad: bfloat16 [32, 16, 3072], P('dp', None, 'mp'), may hold values from -1.5 to 1.5
- norm_gain: float32 [2, 3072], P('segment'), may hold values from 0.1 to 1.9
- master_weights: float32 [2, 12288, 2048], P('segment', 'dp', 'mp'), may hold values from -2 to 2
- first_moment: float32 [2, 12288, 2048], P('segment', 'dp', 'mp'), may hold values from -6 to 6
- second_moment: float32 [2, 12288, 2048], P('segment', 'dp', 'mp'), may hold values from 0.01 to 1
Outputs:
- new_master: float32 [2, 12288, 2048], P('segment', 'dp', 'mp')
- new_first: float32 [2, 12288, 2048], P('segment', 'dp', 'mp')
- new_second: float32 [2, 12288, 2048], P('segment', 'dp', 'mp')
Inputs may be any that keep to these rules, and one draw needn't show every extreme that they name: `visible_index`: in each volume the 16 indices are distinct and increasing.
All inputs are finite; a program needn't handle non-finite values.
Results may differ from a plain program's by a relative error of at most 0.02.
Values may be sent and summed in bfloat16 or wider, within the bound.
A program may use at most 192 MiB of HBM per device.

v0:
```python
import math
import jax
import jax.numpy as jnp
from jax import lax
from jax.sharding import PartitionSpec as P

HD = 128
MB_VOLS = 2
beta_one = 0.9
beta_two = 0.95
learn_rate = 0.01
decay_rate = 0.1
adam_eps = 1e-08
norm_eps = 1e-05
step_count = 10


def from_behind(array, axis, by):
    peers = lax.axis_size(axis)
    pairs = [(i, i + by) for i in range(peers) if 0 <= i + by < peers]
    return lax.ppermute(array, axis, pairs)


def position_table(visible_index, model_width):
    half_width = model_width // 2
    angle_rate = jnp.exp(
        jnp.arange(half_width, dtype=jnp.float32) * (-2.0 * math.log(10000.0) / model_width)
    )
    angles = visible_index.astype(jnp.float32)[..., None] * angle_rate
    return jnp.concatenate([jnp.sin(angles), jnp.cos(angles)], axis=-1)


def norm_forward(hidden, norm_scale):
    values = hidden.astype(jnp.float32)
    centred = values - jnp.mean(values, axis=-1, keepdims=True)
    inverse_dev = lax.rsqrt(jnp.mean(centred * centred, axis=-1, keepdims=True) + norm_eps)
    standard = centred * inverse_dev
    return ((standard * norm_scale).astype(jnp.bfloat16), standard, inverse_dev)


def norm_backward(d_normed, d_output, standard, inverse_dev, norm_scale):
    scaled = d_normed * norm_scale
    inner = (
        scaled
        - jnp.mean(scaled, axis=-1, keepdims=True)
        - standard * jnp.mean(scaled * standard, axis=-1, keepdims=True)
    )
    return (d_output.astype(jnp.float32) + inner * inverse_dev).astype(jnp.bfloat16)


def softmax_rows(scores):
    lifted = jnp.exp(scores - jnp.max(scores, axis=-1, keepdims=True))
    return lifted / jnp.sum(lifted, axis=-1, keepdims=True)


def rounded(values):
    return lax.optimization_barrier(values.astype(jnp.bfloat16)).astype(jnp.float32)


def adam_update(gradient, master, first_moment, second_moment):
    new_first = beta_one * first_moment + (1.0 - beta_one) * gradient
    new_second = beta_two * second_moment + (1.0 - beta_two) * gradient * gradient
    direction = (
        new_first
        / (1.0 - beta_one**step_count)
        / (jnp.sqrt(new_second / (1.0 - beta_two**step_count)) + adam_eps)
    )
    new_master = master - learn_rate * (direction + decay_rate * master)
    return (new_master, new_first, new_second)


def layer_local(layer_in, norm_scale, weights):
    row_count, model_width = layer_in.shape
    col_count = weights.shape[1]
    head_count = col_count // HD
    length = row_count // MB_VOLS
    normed, standard, inverse_dev = norm_forward(layer_in, norm_scale)
    triple = weights[: 3 * model_width].reshape(3, model_width, col_count)
    project = jnp.einsum("nd,sdc->nsc", normed, triple, preferred_element_type=jnp.float32).astype(
        jnp.bfloat16
    )
    shaped = project.reshape(MB_VOLS, length, 3, head_count, HD)
    scores = jnp.einsum(
        "vqhe,vkhe->vhqk", shaped[:, :, 0], shaped[:, :, 1], preferred_element_type=jnp.float32
    ) * (1.0 / math.sqrt(HD))
    softmaxed = softmax_rows(scores)
    probs_half = softmaxed.astype(jnp.bfloat16)
    attended = jnp.einsum(
        "vhqk,vkhe->vqhe", probs_half, shaped[:, :, 2], preferred_element_type=jnp.float32
    )
    attended = attended.astype(jnp.bfloat16).reshape(row_count, col_count)
    return (normed, standard, inverse_dev, project, softmaxed, probs_half, attended)


def head_terms(attended, weights, model_width):
    return rounded(
        jnp.einsum(
            "nc,dc->nd", attended, weights[3 * model_width :], preferred_element_type=jnp.float32
        )
    )


def attention_back(d_output, saved_vals, weights):
    project, softmaxed, probs_half = (saved_vals[3], saved_vals[4], saved_vals[5])
    row_count, model_width = d_output.shape
    col_count = weights.shape[1]
    head_count = col_count // HD
    length = row_count // MB_VOLS
    shaped = project.reshape(MB_VOLS, length, 3, head_count, HD)
    d_attended = jnp.einsum(
        "nd,dc->nc", d_output, weights[3 * model_width :], preferred_element_type=jnp.float32
    )
    d_attended = d_attended.astype(jnp.bfloat16).reshape(MB_VOLS, length, head_count, HD)
    d_probs = jnp.einsum(
        "vqhe,vkhe->vhqk", d_attended, shaped[:, :, 2], preferred_element_type=jnp.float32
    )
    d_scores = (
        softmaxed
        * (d_probs - jnp.sum(d_probs * softmaxed, axis=-1, keepdims=True))
        * (1.0 / math.sqrt(HD))
    ).astype(jnp.bfloat16)
    d_queries = jnp.einsum(
        "vhqk,vkhe->vqhe", d_scores, shaped[:, :, 1], preferred_element_type=jnp.float32
    ).astype(jnp.bfloat16)
    d_keys = jnp.einsum(
        "vhqk,vqhe->vkhe", d_scores, shaped[:, :, 0], preferred_element_type=jnp.float32
    ).astype(jnp.bfloat16)
    d_values = jnp.einsum(
        "vhqk,vqhe->vkhe", probs_half, d_attended, preferred_element_type=jnp.float32
    ).astype(jnp.bfloat16)
    return jnp.stack([d_queries, d_keys, d_values], axis=2).reshape(row_count, 3, col_count)


def feature_terms(d_project, weights, model_width):
    col_count = weights.shape[1]
    triple = weights[: 3 * model_width].reshape(3, model_width, col_count)
    return rounded(jnp.einsum("nsc,sdc->nd", d_project, triple, preferred_element_type=jnp.float32))


def shards(
    patch_tokens, visible_index, output_grad, norm_gain, master_weights, first_moment, second_moment
):
    model_width = patch_tokens.shape[2] * lax.axis_size("mp")
    rows_here = master_weights.shape[1]
    is_first = lax.axis_index("segment") == 0
    norm_scale = norm_gain[0]
    weights = lax.all_gather(master_weights[0].astype(jnp.bfloat16), "dp", axis=0, tiled=True)
    tokens_full, grads_full = (
        lax.all_gather(patch_tokens, "mp", axis=2, tiled=True),
        lax.all_gather(output_grad, "mp", axis=2, tiled=True),
    )
    vol_count, length = visible_index.shape
    micro_count = vol_count // MB_VOLS
    mb_rows = MB_VOLS * length
    first_inputs = (
        tokens_full.astype(jnp.float32) + position_table(visible_index, model_width)
    ).astype(jnp.bfloat16)
    first_inputs = first_inputs.reshape(micro_count, mb_rows, model_width)
    out_grads = grads_full.reshape(micro_count, mb_rows, model_width)
    zeros_full = jnp.zeros((mb_rows, model_width), jnp.bfloat16)
    saved_ticks = []
    received = zeros_full
    for step_index in range(micro_count + 1):
        arriving = received
        own_input = first_inputs[step_index] if step_index < micro_count else zeros_full
        layer_in = jnp.where(is_first, own_input, arriving)
        saved_vals = layer_local(layer_in, norm_scale, weights)
        saved_ticks.append(saved_vals)
        if step_index < micro_count:
            head_part = head_terms(saved_vals[6], weights, model_width)
            mixed = lax.psum(head_part.astype(jnp.bfloat16), "mp").astype(jnp.float32)
            layer_out = (layer_in.astype(jnp.float32) + mixed).astype(jnp.bfloat16)
            received = from_behind(layer_out, "segment", 1)
    back_ticks = []
    for step_index in range(micro_count + 1):
        arriving = received if step_index > 0 else zeros_full
        own_grad = (
            out_grads[micro_count - 1 - step_index] if step_index < micro_count else zeros_full
        )
        d_output = jnp.where(is_first, arriving, own_grad)
        saved_vals = saved_ticks[micro_count - step_index]
        d_project = attention_back(d_output, saved_vals, weights)
        back_ticks.append((d_output, d_project))
        if step_index < micro_count:
            d_terms = feature_terms(d_project, weights, model_width)
            standard, inverse_dev = (saved_vals[1], saved_vals[2])
            summed = lax.psum(d_terms.astype(jnp.bfloat16), "mp").astype(jnp.float32)
            d_input = norm_backward(summed, d_output, standard, inverse_dev, norm_scale)
            received = from_behind(d_input, "segment", -1)
    all_steps = range(micro_count + 1)
    normed_ticks = jnp.stack([saved_ticks[micro_count - step_index][0] for step_index in all_steps])
    attended_ticks = jnp.stack(
        [saved_ticks[micro_count - step_index][6] for step_index in all_steps]
    )
    d_output_ticks = jnp.stack([back_ticks[step_index][0] for step_index in all_steps])
    d_project_ticks = jnp.stack([back_ticks[step_index][1] for step_index in all_steps])
    right_ticks = jnp.concatenate([d_project_ticks, attended_ticks[:, :, None]], axis=2)

    def pick_valid(ticks):
        chosen = jnp.where(is_first, ticks[1:], ticks[:-1])
        return chosen.reshape((micro_count * mb_rows,) + ticks.shape[2:])

    normed_all = pick_valid(normed_ticks)
    d_output_all = pick_valid(d_output_ticks)
    right_all = pick_valid(right_ticks)

    def one_piece(piece_index):
        first_row = piece_index * rows_here
        part_index = first_row // model_width
        col_offset = first_row % model_width
        left_norm = lax.dynamic_slice_in_dim(normed_all, col_offset, rows_here, 1)
        left_grad = lax.dynamic_slice_in_dim(d_output_all, col_offset, rows_here, 1)
        left_side = jnp.where(part_index == 3, left_grad, left_norm)
        right_side = lax.dynamic_index_in_dim(right_all, part_index, 1, keepdims=False)
        return jnp.einsum("tr,tc->rc", left_side, right_side, preferred_element_type=jnp.float32)

    blocks = lax.map(
        one_piece, jnp.arange(rows_here * lax.axis_size("dp") // rows_here, dtype=jnp.int32)
    )
    gradient = lax.psum_scatter(
        blocks.reshape(rows_here * lax.axis_size("dp"), blocks.shape[2]).astype(jnp.bfloat16),
        "dp",
        scatter_dimension=0,
        tiled=True,
    ).astype(jnp.float32)
    new_master, new_first, new_second = adam_update(
        gradient, master_weights[0], first_moment[0], second_moment[0]
    )
    return (new_master[None], new_first[None], new_second[None])


def solution(mesh):
    placed = (
        P("dp", None, "mp"),
        P("dp", None),
        P("dp", None, "mp"),
        P("segment", None),
        P("segment", "dp", "mp"),
        P("segment", "dp", "mp"),
        P("segment", "dp", "mp"),
    )
    return jax.shard_map(
        shards,
        mesh=mesh,
        in_specs=placed,
        out_specs=(P("segment", "dp", "mp"), P("segment", "dp", "mp"), P("segment", "dp", "mp")),
        check_vma=False,
    )
```

profile of v0, /device:TPU:0, one launch (start us, length us, event | category | flops | bytes accessed | tf_op | source)
XLA Modules:
  0.0 909.8 jit_solution(2568975783798834956)
XLA Ops:
  7.2 4.9 bitcast_convert_fusion
  12.3 10.1 %all_gather.10 = bf16[8,16,3072]{2,1,0:T(8,128)(2,1)S(1)} all-gather(bf16[8,16,768]{2,1,0:T(8,128)(2,1)S(1)} %copy-done.3), channel_id=1, replica_groups=mesh['segment'=2,'dp'=4,'mp'=4] {'mp'}, dimensions={2}, use_global_device_ids=true | all-gather | bytes 983040 | tf_op jit(solution)/shard_map/all_gather | solution.py:149
  25.8 207.5 %all-gather.2.cloned.1.call-done = bf16[12288,512]{1,0:T(8,128)(2,1)} async-done(((bf16[3072,512]{1,0:T(8,128)(2,1)}), bf16[12288,512]{1,0:T(8,128)(2,1)}) %all-gather.2.cloned.1.call-update) | async-done | bytes 12582928 | tf_op jit(solution)/shard_map/all_gather | solution.py:147
  233.2 5.2 slice.160
  244.9 3.6 convolution_convert_fusion.3
  248.6 30.0 %all-reduce.9.cloned.1.call-done = bf16[32,3072]{1,0:T(8,128)(2,1)} async-done(((bf16[32,3072]{1,0:T(8,128)(2,1)}), bf16[32,3072]{1,0:T(8,128)(2,1)}) %all-reduce.9.cloned.1.call-update) | async-done | bytes 196624 | tf_op jit(solution)/shard_map/psum | solution.py:171
  286.6 5.5 convolution_convert_fusion.7
  293.3 3.6 convolution_convert_fusion.2
  297.0 33.0 %all-reduce.11.cloned.1.call-done = bf16[32,3072]{1,0:T(8,128)(2,1)} async-done(((bf16[32,3072]{1,0:T(8,128)(2,1)}), bf16[32,3072]{1,0:T(8,128)(2,1)}) %all-reduce.11.cloned.1.call-update) | async-done | bytes 196624 | tf_op jit(solution)/shard_map/psum | solution.py:171
  337.9 5.5 convolution_convert_fusion.6
  344.7 3.6 convolution_convert_fusion.1
  348.4 7.8 all_gather.9
  356.2 25.1 %all-reduce.13.cloned.1.call-done = bf16[32,3072]{1,0:T(8,128)(2,1)} async-done(((bf16[32,3072]{1,0:T(8,128)(2,1)}), bf16[32,3072]{1,0:T(8,128)(2,1)}) %all-reduce.13.cloned.1.call-update) | async-done | bytes 196624 | tf_op jit(solution)/shard_map/psum | solution.py:171
  389.3 5.5 convolution_convert_fusion.5
  395.4 3.6 convolution_convert_fusion
  399.8 32.2 %all-reduce.15.cloned.1.call-done = bf16[32,3072]{1,0:T(8,128)(2,1)} async-done(((bf16[32,3072]{1,0:T(8,128)(2,1)}), bf16[32,3072]{1,0:T(8,128)(2,1)}) %all-reduce.15.cloned.1.call-update) | async-done | bytes 196624 | tf_op jit(solution)/shard_map/psum | solution.py:171
  440.0 5.5 convolution_convert_fusion.4
  446.7 7.2 fusion.21
  456.2 30.7 %all-reduce.17.cloned.1.call-done = bf16[32,3072]{1,0:T(8,128)(2,1)} async-done(((bf16[32,3072]{1,0:T(8,128)(2,1)}), bf16[32,3072]{1,0:T(8,128)(2,1)}) %all-reduce.17.cloned.1.call-update) | async-done | bytes 196624 | tf_op jit(solution)/shard_map/psum | solution.py:187
  490.5 6.2 collective-permute-done.4
  500.4 7.2 fusion.22
  507.7 31.0 %all-reduce.19.cloned.1.call-done = bf16[32,3072]{1,0:T(8,128)(2,1)} async-done(((bf16[32,3072]{1,0:T(8,128)(2,1)}), bf16[32,3072]{1,0:T(8,128)(2,1)}) %all-reduce.19.cloned.1.call-update) | async-done | bytes 196624 | tf_op jit(solution)/shard_map/psum | solution.py:187
  542.4 6.2 collective-permute-done.5
  552.2 7.2 fusion.23
  559.6 30.9 %all-reduce.21.cloned.1.call-done = bf16[32,3072]{1,0:T(8,128)(2,1)} async-done(((bf16[32,3072]{1,0:T(8,128)(2,1)}), bf16[32,3072]{1,0:T(8,128)(2,1)}) %all-reduce.21.cloned.1.call-update) | async-done | bytes 196624 | tf_op jit(solution)/shard_map/psum | solution.py:187
  594.5 5.9 collective-permute-done.6
  604.1 7.2 fusion.24
  611.4 31.0 %all-reduce.23.cloned.1.call-done = bf16[32,3072]{1,0:T(8,128)(2,1)} async-done(((bf16[32,3072]{1,0:T(8,128)(2,1)}), bf16[32,3072]{1,0:T(8,128)(2,1)}) %all-reduce.23.cloned.1.call-update) | async-done | bytes 196624 | tf_op jit(solution)/shard_map/psum | solution.py:187
  646.3 6.1 collective-permute-done.7
  659.7 15.8 %while.12 = (s32[]{:T(128)}, bf16[4,3072,512]{2,1,0:T(8,128)(2,1)}, s32[4]{0:T(128)S(1)}, bf16[128,3072]{1,0:T(8,128)(2,1)S(1)}, bf16[128,3072]{1,0:T(8,128)(2,1...) while((s32[]{:T(128)}, bf16[4,3072,512]{2,1,0:T(8,128)(2,1)}, ...), condition=%wide.region_42.43_spmd, body=%wide.region_41.42_spmd.sunk | while | flops 403046400 | bytes 7996187 | solution.py:217
  675.5 211.3 %reduce-scatter.2.cloned.1.call-done = bf16[3072,512]{1,0:T(8,128)(2,1)} async-done(((bf16[12288,512]{1,0:T(8,128)(2,1)}), bf16[3072,512]{1,0:T(8,128)(2,1)}) %reduce-scatter.2.cloned.1.call-update) | async-done | bytes 3145744 | tf_op jit(solution)/shard_map/reduce_scatter | solution.py:220
  886.8 16.1 %fusion.25 = (f32[1,3072,512]{2,1,0:T(8,128)}, f32[1,3072,512]{2,1,0:T(8,128)}, f32[1,3072,512]{2,1,0:T(8,128)}) fusion(bf16[3072,512]{1,0:T(8,128)(2,1)} %reduce-scatter.2.cloned.1.call-done, f32[1,3072,512]{2,1,0:T(8,128)} %param.15, f32[1,3072,512]{2,1,0:T(8,128)} %param.14, f32[1,3072,512]{2,1,0:T(8,128)} %param.13), kind=kLoop, calls=%fused_computation.39 | loop fusion | flops 25165824 | bytes 40894464 | tf_op jit(solution)/shard_map/broadcast_in_dim | solution.py:229
  (284 shorter events, 95.3 us)
Async XLA Ops:
  7.2 226.1 %all-gather.2.cloned.1.call-start = ((), (), s32[]{:S(2)}) async-start(), calls=%async_computation.1 | async-start | bytes 15728640 | tf_op jit(solution)/shard_map/all_gather | solution.py:147
  12.2 266.4 %all-reduce.9.cloned.1.call-start = ((), (), s32[]{:S(2)}) async-start(), calls=%async_computation.2 | async-start | bytes 393216 | tf_op jit(solution)/shard_map/psum | solution.py:171
  248.5 81.4 %all-reduce.11.cloned.1.call-start = ((), (), s32[]{:S(2)}) async-start(), calls=%async_computation.3 | async-start | bytes 393216 | tf_op jit(solution)/shard_map/psum | solution.py:171
  279.6 6.6 collective-permute-start
  292.9 44.7 %copy-start.32 = (f32[2,4,16]{2,1,0:T(4,128)}, f32[2,4,16]{2,1,0:T(4,128)S(1)}, u32[]{:S(2)}) copy-start(f32[2,4,16]{2,1,0:T(4,128)S(1)} %get-tuple-element.142) | copy-start | bytes 1540
  296.9 84.4 %all-reduce.13.cloned.1.call-start = ((), (), s32[]{:S(2)}) async-start(), calls=%async_computation.4 | async-start | bytes 393216 | tf_op jit(solution)/shard_map/psum | solution.py:171
  330.9 6.6 collective-permute-start.1
  348.3 83.8 %all-reduce.15.cloned.1.call-start = ((), (), s32[]{:S(2)}) async-start(), calls=%async_computation.5 | async-start | bytes 393216 | tf_op jit(solution)/shard_map/psum | solution.py:171
  382.3 6.6 collective-permute-start.2
  399.0 87.9 %all-reduce.17.cloned.1.call-start = ((), (), s32[]{:S(2)}) async-start(), calls=%async_computation.6 | async-start | bytes 393216 | tf_op jit(solution)/shard_map/psum | solution.py:187
  433.0 6.6 collective-permute-start.3
  453.9 84.9 %all-reduce.19.cloned.1.call-start = ((), (), s32[]{:S(2)}) async-start(), calls=%async_computation.7 | async-start | bytes 393216 | tf_op jit(solution)/shard_map/psum | solution.py:187
  489.2 7.6 collective-permute-start.4
  500.4 50.9 %copy-start.14 = (bf16[2,16,1,4,128]{4,3,1,0,2:T(4,128)(2,1)S(1)}, bf16[2,16,1,4,128]{4,3,1,0,2:T(4,128)(2,1)}, u32[]{:S(2)}) copy-start(bf16[2,16,1,4,128]{4,3,1,0,2:T(4,128)(2,1)} %copy-done.13) | copy-start | bytes 98308
  500.4 51.0 %copy-start.24 = (bf16[2,16,1,4,128]{4,3,1,0,2:T(4,128)(2,1)S(1)}, bf16[2,16,1,4,128]{4,3,1,0,2:T(4,128)(2,1)}, u32[]{:S(2)}) copy-start(bf16[2,16,1,4,128]{4,3,1,0,2:T(4,128)(2,1)} %copy-done.23) | copy-start | bytes 98308
  500.4 51.0 %copy-start.29 = (f32[2,4,16,16]{2,3,1,0:T(8,128)S(1)}, f32[2,4,16,16]{2,3,1,0:T(8,128)}, u32[]{:S(2)}) copy-start(f32[2,4,16,16]{2,3,1,0:T(8,128)} %get-tuple-element.145) | copy-start | bytes 24580
  500.4 51.0 %copy-start.35 = (f32[2,4,16]{2,1,0:T(4,128)S(1)}, f32[2,4,16]{2,1,0:T(4,128)}, u32[]{:S(2)}) copy-start(f32[2,4,16]{2,1,0:T(4,128)} %copy-done.34) | copy-start | bytes 1540
  507.6 44.0 %copy-start.26 = (bf16[2,16,1,4,128]{4,3,1,0,2:T(4,128)(2,1)S(1)}, bf16[2,16,1,4,128]{4,3,1,0,2:T(4,128)(2,1)}, u32[]{:S(2)}) copy-start(bf16[2,16,1,4,128]{4,3,1,0,2:T(4,128)(2,1)} %copy-done.25) | copy-start | bytes 98308
  507.7 82.9 %all-reduce.21.cloned.1.call-start = ((), (), s32[]{:S(2)}) async-start(), calls=%async_computation.8 | async-start | bytes 393216 | tf_op jit(solution)/shard_map/psum | solution.py:187
  541.1 7.6 collective-permute-start.5
  559.4 43.8 %copy-start.20 = (bf16[2,16,1,4,128]{4,3,1,0,2:T(4,128)(2,1)S(1)}, bf16[2,16,1,4,128]{4,3,1,0,2:T(4,128)(2,1)}, u32[]{:S(2)}) copy-start(bf16[2,16,1,4,128]{4,3,1,0,2:T(4,128)(2,1)} %copy-done.19) | copy-start | bytes 98308
  559.4 43.8 %copy-start.28 = (f32[2,4,16,16]{2,3,1,0:T(8,128)S(1)}, f32[2,4,16,16]{2,3,1,0:T(8,128)}, u32[]{:S(2)}) copy-start(f32[2,4,16,16]{2,3,1,0:T(8,128)} %get-tuple-element.143) | copy-start | bytes 24580
  559.4 43.8 %copy-start.33 = (f32[2,4,16]{2,1,0:T(4,128)S(1)}, f32[2,4,16]{2,1,0:T(4,128)}, u32[]{:S(2)}) copy-start(f32[2,4,16]{2,1,0:T(4,128)} %copy-done.32) | copy-start | bytes 1540
  559.4 44.0 %copy-start.22 = (bf16[2,16,1,4,128]{4,3,1,0,2:T(4,128)(2,1)S(1)}, bf16[2,16,1,4,128]{4,3,1,0,2:T(4,128)(2,1)}, u32[]{:S(2)}) copy-start(bf16[2,16,1,4,128]{4,3,1,0,2:T(4,128)(2,1)} %copy-done.21) | copy-start | bytes 98308
  559.5 83.0 %all-reduce.23.cloned.1.call-start = ((), (), s32[]{:S(2)}) async-start(), calls=%async_computation.9 | async-start | bytes 393216 | tf_op jit(solution)/shard_map/psum | solution.py:187
  592.9 7.6 collective-permute-start.6
  611.3 44.3 %copy-start.10 = (bf16[2,16,1,4,128]{4,3,1,0,2:T(4,128)(2,1)S(1)}, bf16[2,16,1,4,128]{4,3,1,0,2:T(4,128)(2,1)}, u32[]{:S(2)}) copy-start(bf16[2,16,1,4,128]{4,3,1,0,2:T(4,128)(2,1)} %copy-done.9) | copy-start | bytes 98308
  611.3 44.4 %copy-start.16 = (bf16[2,16,1,4,128]{4,3,1,0,2:T(4,128)(2,1)S(1)}, bf16[2,16,1,4,128]{4,3,1,0,2:T(4,128)(2,1)}, u32[]{:S(2)}) copy-start(bf16[2,16,1,4,128]{4,3,1,0,2:T(4,128)(2,1)} %copy-done.15) | copy-start | bytes 98308
  611.3 44.4 %copy-start.31 = (f32[2,4,16]{2,1,0:T(4,128)S(1)}, f32[2,4,16]{2,1,0:T(4,128)}, u32[]{:S(2)}) copy-start(f32[2,4,16]{2,1,0:T(4,128)} %copy-done.30) | copy-start | bytes 1540
  611.3 45.6 %copy-start.18 = (bf16[2,16,1,4,128]{4,3,1,0,2:T(4,128)(2,1)S(1)}, bf16[2,16,1,4,128]{4,3,1,0,2:T(4,128)(2,1)}, u32[]{:S(2)}) copy-start(bf16[2,16,1,4,128]{4,3,1,0,2:T(4,128)(2,1)} %copy-done.17) | copy-start | bytes 98308
  611.3 275.4 %reduce-scatter.2.cloned.1.call-start = ((), (), s32[]{:S(2)}) async-start(), calls=%async_computation.10 | async-start | bytes 15728640 | tf_op jit(solution)/shard_map/reduce_scatter | solution.py:220
  644.8 7.6 collective-permute-start.7
  (22 other events, 520.8 us)
Sparse Core Ops, SparseCore 0:
  12.3 220.9 all-gather.1
  248.7 29.8 all-reduce.8
  297.0 32.8 all-reduce.10
  348.4 32.8 all-reduce.12
  399.1 32.8 all-reduce.14
  454.0 32.8 all-reduce.16
  507.8 30.9 all-reduce.18
  559.6 30.9 all-reduce.20
  611.5 30.9 all-reduce.22
  675.6 211.1 reduce-scatter.1
where the time goes:
time: 911 us; the launch traced here: 910 us
  waiting for transfers between devices  697 us (77%)
  matrix products  100 us (11%)
  other arithmetic  41.1 us (5%)
  starting transfers between devices  19.5 us (2%)
  blocking collectives  17.9 us (2%)
  local copies, waits for them, and re-layouts  16 us (2%)
  between operations  15.4 us (2%)
    reduce_scatter x1, waiting for transfers between devices, shards(): lax.psum_scatter(blocks.reshape(rows_here * lax.axis_size('dp'), blocks.s...  211 us
    all_gather x1, waiting for transfers between devices, shards(): lax.all_gather(master_weights[0].astype(jnp.bfloat16), 'dp', axis=0, tile...  207 us
    psum x4, waiting for transfers between devices, shards(): summed = lax.psum(d_terms.astype(jnp.bfloat16), 'mp').astype(jnp.float32)  124 us
    psum x4, waiting for transfers between devices, shards(): mixed = lax.psum(head_part.astype(jnp.bfloat16), 'mp').astype(jnp.float32)  120 us
    ppermute x8, waiting for transfers between devices, from_behind(): return lax.ppermute(array, axis, pairs)  34 us
    dot_general x4, matrix products, feature_terms(): jnp.einsum('nsc,sdc->nd', d_project, triple, preferred_element_type=jnp.f...  28.8 us
    dot_general x5, matrix products, layer_local(): jnp.einsum('nd,sdc->nsc', normed, triple, preferred_element_type=jnp.floa...  23.5 us
    ppermute x8, starting transfers between devices, from_behind(): return lax.ppermute(array, axis, pairs)  19.1 us
  transfers between devices with their start and end apart: 18, of which 18 were waited for; matrix products, arithmetic and copies ran while one was open for 1% of the time, Pallas kernels for 0%

commit v1 on v0

--- a/solution.py
+++ b/solution.py
@@ -15,6 +15,24 @@
 step_count = 10
 
 
+def laid_out(pieces, dim):
+    pieces = jnp.moveaxis(pieces, 0, dim)
+    shape = pieces.shape
+    return pieces.reshape(*shape[:dim], shape[dim] * shape[dim + 1], *shape[dim + 2 :])
+
+
+def collected_by_bits(shard, axis):
+    size = lax.axis_size(axis)
+    blocks = shard[None]
+    for level in range(size.bit_length() - 1):
+        bit = 1 << level
+        other = lax.ppermute(blocks, axis, [(i, i ^ bit) for i in range(size)])
+        both = jnp.stack([blocks, other])
+        upper = lax.axis_index(axis) >> level & 1
+        blocks = jnp.where(upper == 0, both, both[::-1]).reshape(-1, *shard.shape)
+    return blocks
+
+
 def from_behind(array, axis, by):
     peers = lax.axis_size(axis)
     pairs = [(i, i + by) for i in range(peers) if 0 <= i + by < peers]
@@ -144,7 +162,8 @@
     rows_here = master_weights.shape[1]
     is_first = lax.axis_index("segment") == 0
     norm_scale = norm_gain[0]
-    weights = lax.all_gather(master_weights[0].astype(jnp.bfloat16), "dp", axis=0, tiled=True)
+    array_2 = master_weights[0].astype(jnp.bfloat16)
+    weights = laid_out(collected_by_bits(array_2, "dp"), 0)
     tokens_full, grads_full = (
         lax.all_gather(patch_tokens, "mp", axis=2, tiled=True),
         lax.all_gather(output_grad, "mp", axis=2, tiled=True),

time: 911 us -> 1050 us (1.15)
  waiting for transfers between devices: 697 us -> 815 us
  other arithmetic: 41.1 us -> 65.1 us
    ppermute x0 -> x2, waiting for transfers between devices: none -> 323 us  [collected_by_bits(): other = lax.ppermute(blocks, axis, [(i, i ^ bit) for i in range(size)])]
    all_gather x1 -> x0, waiting for transfers between devices: 207 us -> none  [shards(): lax.all_gather(master_weights[0].astype(jnp.bfloat16), 'dp', axis=0, tile...]
    another operation x0 -> x3, other arithmetic: none -> 13.7 us  [collected_by_bits(): both = jnp.stack([blocks, other])]
  transfers between devices with their start and end apart: 18 -> 19, of which waited for: 18 -> 19; matrix products, arithmetic and copies ran while one was open for 1% -> 1% of each run, Pallas kernels for 0% -> 0%
where the time goes in v1:
time: 1050 us
  waiting for transfers between devices  815 us (78%)
  matrix products  98.3 us (9%)
  other arithmetic  65.1 us (6%)
  starting transfers between devices  25.3 us (2%)
  blocking collectives  16.6 us (2%)
  between operations  14.8 us (1%)
  local copies, waits for them, and re-layouts  13.9 us (1%)
    ppermute x2, waiting for transfers between devices, collected_by_bits(): other = lax.ppermute(blocks, axis, [(i, i ^ bit) for i in range(size)])  323 us
    reduce_scatter x1, waiting for transfers between devices, shards(): lax.psum_scatter(blocks.reshape(rows_here * lax.axis_size('dp'), blocks.s...  211 us
    psum x4, waiting for transfers between devices, shards(): summed = lax.psum(d_terms.astype(jnp.bfloat16), 'mp').astype(jnp.float32)  125 us
    psum x4, waiting for transfers between devices, shards(): mixed = lax.psum(head_part.astype(jnp.bfloat16), 'mp').astype(jnp.float32)  124 us
    ppermute x8, waiting for transfers between devices, from_behind(): return lax.ppermute(array, axis, pairs)  32.1 us
    dot_general x4, matrix products, feature_terms(): jnp.einsum('nsc,sdc->nd', d_project, triple, preferred_element_type=jnp.f...  28.8 us
    dot_general x5, matrix products, layer_local(): jnp.einsum('nd,sdc->nsc', normed, triple, preferred_element_type=jnp.floa...  23.5 us
  transfers between devices with their start and end apart: 19, of which 19 were waited for; matrix products, arithmetic and copies ran while one was open for 1% of the time, Pallas kernels for 0%

profile of v1, /device:TPU:0, one launch (start us, length us, event | category | flops | bytes accessed | tf_op | source)
XLA Modules:
  0.0 1051.6 jit_solution(12105122791192166408)
XLA Ops:
  7.2 4.9 convert_element_type.387
  18.3 65.1 %collective-permute-done = bf16[1,3072,512]{2,1,0:T(8,128)(2,1)S(1)} collective-permute-done((bf16[1,3072,512]{2,1,0:T(8,128)(2,1)}, bf16[1,3072,512]{2,1,0:T(8,128)(2,1)S(1)}, u32[]{:S(2)}, u32[]{:S(2)}) %collective-permute-start) | collective-permute-done | bytes 3145760 | tf_op jit(solution)/shard_map/ppermute | solution.py:29
  87.6 6.5 fusion.21
  96.8 8.8 all_gather.7
  109.0 257.8 %collective-permute-done.1 = bf16[2,3072,512]{2,1,0:T(8,128)(2,1)} collective-permute-done((bf16[2,3072,512]{2,1,0:T(8,128)(2,1)}, bf16[2,3072,512]{2,1,0:T(8,128)(2,1)}, u32[]{:S(2)}, u32[]{:S(2)}) %collective-permute-start.1) | collective-permute-done | bytes 6291488 | tf_op jit(solution)/shard_map/ppermute | solution.py:29
  366.8 4.7 pad_maximum_fusion
  371.5 3.6 reverse_select_fusion
  375.9 3.9 copy-done.1
  389.9 32.8 %all-reduce.9.cloned.1.call-done = bf16[32,3072]{1,0:T(8,128)(2,1)} async-done(((bf16[32,3072]{1,0:T(8,128)(2,1)}), bf16[32,3072]{1,0:T(8,128)(2,1)}) %all-reduce.9.cloned.1.call-update) | async-done | bytes 196624 | tf_op jit(solution)/shard_map/psum | solution.py:190
  430.6 5.5 convolution_convert_fusion.7
  441.0 33.0 %all-reduce.11.cloned.1.call-done = bf16[32,3072]{1,0:T(8,128)(2,1)} async-done(((bf16[32,3072]{1,0:T(8,128)(2,1)}), bf16[32,3072]{1,0:T(8,128)(2,1)}) %all-reduce.11.cloned.1.call-update) | async-done | bytes 196624 | tf_op jit(solution)/shard_map/psum | solution.py:190
  481.9 5.5 convolution_convert_fusion.6
  492.3 7.8 all_gather.6
  500.2 25.1 %all-reduce.13.cloned.1.call-done = bf16[32,3072]{1,0:T(8,128)(2,1)} async-done(((bf16[32,3072]{1,0:T(8,128)(2,1)}), bf16[32,3072]{1,0:T(8,128)(2,1)}) %all-reduce.13.cloned.1.call-update) | async-done | bytes 196624 | tf_op jit(solution)/shard_map/psum | solution.py:190
  533.3 5.5 convolution_convert_fusion.5
  543.2 32.8 %all-reduce.15.cloned.1.call-done = bf16[32,3072]{1,0:T(8,128)(2,1)} async-done(((bf16[32,3072]{1,0:T(8,128)(2,1)}), bf16[32,3072]{1,0:T(8,128)(2,1)}) %all-reduce.15.cloned.1.call-update) | async-done | bytes 196624 | tf_op jit(solution)/shard_map/psum | solution.py:190
  583.9 5.5 convolution_convert_fusion.4
  590.6 7.2 fusion.23
  598.3 32.5 %all-reduce.17.cloned.1.call-done = bf16[32,3072]{1,0:T(8,128)(2,1)} async-done(((bf16[32,3072]{1,0:T(8,128)(2,1)}), bf16[32,3072]{1,0:T(8,128)(2,1)}) %all-reduce.17.cloned.1.call-update) | async-done | bytes 196624 | tf_op jit(solution)/shard_map/psum | solution.py:206
  634.5 6.2 collective-permute-done.6
  644.3 7.2 fusion.24
  651.6 31.0 %all-reduce.19.cloned.1.call-done = bf16[32,3072]{1,0:T(8,128)(2,1)} async-done(((bf16[32,3072]{1,0:T(8,128)(2,1)}), bf16[32,3072]{1,0:T(8,128)(2,1)}) %all-reduce.19.cloned.1.call-update) | async-done | bytes 196624 | tf_op jit(solution)/shard_map/psum | solution.py:206
  687.1 5.4 collective-permute-done.7
  696.1 7.2 fusion.25
  703.4 31.0 %all-reduce.21.cloned.1.call-done = bf16[32,3072]{1,0:T(8,128)(2,1)} async-done(((bf16[32,3072]{1,0:T(8,128)(2,1)}), bf16[32,3072]{1,0:T(8,128)(2,1)}) %all-reduce.21.cloned.1.call-update) | async-done | bytes 196624 | tf_op jit(solution)/shard_map/psum | solution.py:206
  739.4 4.9 collective-permute-done.8
  747.9 7.2 fusion.26
  755.8 30.4 %all-reduce.23.cloned.1.call-done = bf16[32,3072]{1,0:T(8,128)(2,1)} async-done(((bf16[32,3072]{1,0:T(8,128)(2,1)}), bf16[32,3072]{1,0:T(8,128)(2,1)}) %all-reduce.23.cloned.1.call-update) | async-done | bytes 196624 | tf_op jit(solution)/shard_map/psum | solution.py:206
  790.1 6.1 collective-permute-done.9
  801.8 15.8 %while.12 = (s32[]{:T(128)}, bf16[4,3072,512]{2,1,0:T(8,128)(2,1)}, s32[4]{0:T(128)S(1)}, bf16[128,3072]{1,0:T(8,128)(2,1)S(1)}, bf16[128,3072]{1,0:T(8,128)(2,1...) while((s32[]{:T(128)}, bf16[4,3072,512]{2,1,0:T(8,128)(2,1)}, ...), condition=%wide.region_42.43_spmd, body=%wide.region_41.42_spmd.sunk | while | flops 403046400 | bytes 7996187 | solution.py:236
  817.6 211.3 %reduce-scatter.2.cloned.1.call-done = bf16[3072,512]{1,0:T(8,128)(2,1)} async-done(((bf16[12288,512]{1,0:T(8,128)(2,1)}), bf16[3072,512]{1,0:T(8,128)(2,1)}) %reduce-scatter.2.cloned.1.call-update) | async-done | bytes 3145744 | tf_op jit(solution)/shard_map/reduce_scatter | solution.py:239
  1028.9 16.1 %fusion.27 = (f32[1,3072,512]{2,1,0:T(8,128)}, f32[1,3072,512]{2,1,0:T(8,128)}, f32[1,3072,512]{2,1,0:T(8,128)}) fusion(bf16[3072,512]{1,0:T(8,128)(2,1)} %reduce-scatter.2.cloned.1.call-done, f32[1,3072,512]{2,1,0:T(8,128)} %param.15, f32[1,3072,512]{2,1,0:T(8,128)} %param.14, f32[1,3072,512]{2,1,0:T(8,128)} %param.13), kind=kLoop, calls=%fused_computation.44 | loop fusion | flops 25165824 | bytes 40894464 | tf_op jit(solution)/shard_map/broadcast_in_dim | solution.py:248
  (240 shorter events, 121.8 us)
Async XLA Ops:
  7.2 415.5 %all-reduce.9.cloned.1.call-start = ((), (), s32[]{:S(2)}) async-start(), calls=%async_computation.1 | async-start | bytes 393216 | tf_op jit(solution)/shard_map/psum | solution.py:190
  12.1 71.3 %collective-permute-start = (bf16[1,3072,512]{2,1,0:T(8,128)(2,1)}, bf16[1,3072,512]{2,1,0:T(8,128)(2,1)S(1)}, u32[]{:S(2)}, u32[]{:S(2)}) collective-permute-start(bf16[1,3072,512]{2,1,0:T(8,128)(2,1)} %convert_element_type.387), channel_id=1, source_target_pairs={{0,4},{4,0},{8,12},{12,8},{1,5},{5,1},{9,13},{13,9},{2,6},{6,2},{1... | collective-permute-start | bytes 9437192 | tf_op jit(solution)/shard_map/ppermute | solution.py:29
  83.4 1.7 copy-start.3
  87.5 9.3 copy-start.7
  87.5 9.3 copy-start.5
  87.5 21.3 %copy-start.4 = (f32[1,3072]{1,0:T(1,128)S(1)}, f32[1,3072]{1,0:T(1,128)}, u32[]{:S(2)}) copy-start(f32[1,3072]{1,0:T(1,128)} %param.12) | copy-start | bytes 36868
  94.0 272.7 %collective-permute-start.1 = (bf16[2,3072,512]{2,1,0:T(8,128)(2,1)}, bf16[2,3072,512]{2,1,0:T(8,128)(2,1)}, u32[]{:S(2)}, u32[]{:S(2)}) collective-permute-start(bf16[2,3072,512]{2,1,0:T(8,128)(2,1)} %get-tuple-element.112), channel_id=1, source_target_pairs={{0,8},{4,12},{8,0},{12,4},{1,9},{5,13},{9,1},{13,5},{2,10},{6,14},... | collective-permute-start | bytes 18874376 | tf_op jit(solution)/shard_map/ppermute | solution.py:29
  96.8 270.0 %copy-start.2 = (bf16[1,2,3072,512]{3,2,1,0:T(8,128)(2,1)S(1)}, bf16[1,2,3072,512]{3,2,1,0:T(8,128)(2,1)}, u32[]{:S(2)}) copy-start(bf16[1,2,3072,512]{3,2,1,0:T(8,128)(2,1)} %get-tuple-element.111) | copy-start | bytes 18874372
  375.2 4.6 copy-start.1
  379.7 3.6 copy-start
  389.8 84.1 %all-reduce.11.cloned.1.call-start = ((), (), s32[]{:S(2)}) async-start(), calls=%async_computation.2 | async-start | bytes 393216 | tf_op jit(solution)/shard_map/psum | solution.py:190
  423.6 6.6 collective-permute-start.2
  440.9 84.4 %all-reduce.13.cloned.1.call-start = ((), (), s32[]{:S(2)}) async-start(), calls=%async_computation.3 | async-start | bytes 393216 | tf_op jit(solution)/shard_map/psum | solution.py:190
  474.9 6.6 collective-permute-start.3
  481.9 10.4 copy-start.6
  492.3 83.7 %all-reduce.15.cloned.1.call-start = ((), (), s32[]{:S(2)}) async-start(), calls=%async_computation.4 | async-start | bytes 393216 | tf_op jit(solution)/shard_map/psum | solution.py:190
  526.3 6.6 collective-permute-start.4
  543.0 87.9 %all-reduce.17.cloned.1.call-start = ((), (), s32[]{:S(2)}) async-start(), calls=%async_computation.5 | async-start | bytes 393216 | tf_op jit(solution)/shard_map/psum | solution.py:206
  577.0 6.6 collective-permute-start.5
  597.8 84.8 %all-reduce.19.cloned.1.call-start = ((), (), s32[]{:S(2)}) async-start(), calls=%async_computation.6 | async-start | bytes 393216 | tf_op jit(solution)/shard_map/psum | solution.py:206
  633.2 7.6 collective-permute-start.6
  644.3 51.0 %copy-start.10 = (f32[2,4,16,16]{2,3,1,0:T(8,128)S(1)}, f32[2,4,16,16]{2,3,1,0:T(8,128)}, u32[]{:S(2)}) copy-start(f32[2,4,16,16]{2,3,1,0:T(8,128)} %get-tuple-element.147) | copy-start | bytes 24580
  651.5 82.9 %all-reduce.21.cloned.1.call-start = ((), (), s32[]{:S(2)}) async-start(), calls=%async_computation.7 | async-start | bytes 393216 | tf_op jit(solution)/shard_map/psum | solution.py:206
  685.0 7.6 collective-permute-start.7
  703.3 43.7 %copy-start.9 = (f32[2,4,16,16]{2,3,1,0:T(8,128)S(1)}, f32[2,4,16,16]{2,3,1,0:T(8,128)}, u32[]{:S(2)}) copy-start(f32[2,4,16,16]{2,3,1,0:T(8,128)} %get-tuple-element.145) | copy-start | bytes 24580
  703.3 82.9 %all-reduce.23.cloned.1.call-start = ((), (), s32[]{:S(2)}) async-start(), calls=%async_computation.8 | async-start | bytes 393216 | tf_op jit(solution)/shard_map/psum | solution.py:206
  736.7 7.6 collective-permute-start.8
  755.1 43.7 %copy-start.8 = (f32[2,4,16,16]{2,3,1,0:T(8,128)S(1)}, f32[2,4,16,16]{2,3,1,0:T(8,128)}, u32[]{:S(2)}) copy-start(f32[2,4,16,16]{2,3,1,0:T(8,128)} %get-tuple-element.143) | copy-start | bytes 24580
  755.1 273.8 %reduce-scatter.2.cloned.1.call-start = ((), (), s32[]{:S(2)}) async-start(), calls=%async_computation.9 | async-start | bytes 15728640 | tf_op jit(solution)/shard_map/reduce_scatter | solution.py:239
  788.6 7.6 collective-permute-start.9
Sparse Core Ops, SparseCore 0:
  389.9 32.6 all-reduce.8
  441.0 32.8 all-reduce.10
  492.4 32.8 all-reduce.12
  543.1 32.8 all-reduce.14
  597.9 32.8 all-reduce.16
  651.6 30.9 all-reduce.18
  703.4 30.9 all-reduce.20
  755.3 30.9 all-reduce.22
  817.8 211.1 reduce-scatter.1
